TPU v7x, 32 devices: a whole 2x2x4 slice. The times are simulated.
32 devices in a mesh: chan: 8 (over z, core), grp: 4 (over y, x).
Axes of the slice: x: 2, y: 2, z: 4, core: 2. Of those that a mesh axis runs over, the one named last changes fastest.
Arguments:
- residual: bfloat16 [128, 4096], P('grp', 'chan'), may hold values from -6 to 6
- conv_input: bfloat16 [128, 8192], P('grp', 'chan'), may hold values from -6 to 6
- gate_input: bfloat16 [128, 8192], P('grp', 'chan'), may hold values from -6 to 6
- conv_state: bfloat16 [128, 3, 8192], P('grp', None, 'chan'), may hold values from -6 to 6
- conv_weight: float32 [4, 8192], P(None, 'chan'), may hold values from -3 to 3
- conv_bias: float32 [8192], P('chan'), may hold values from -1 to 1
- state_proj: bfloat16 [8192, 288], P('chan'), may hold values from -0.0625 to 0.0625
- step_proj: bfloat16 [256, 8192], P(None, 'chan'), may hold values from -0.375 to 0.375
- step_bias: float32 [8192], P('chan'), may hold values from -5 to -1
- decay_rate: float32 [16, 8192], P(None, 'chan'), may hold values from 1 to 16
- skip_gain: float32 [8192], P('chan'), may hold values from 0.5 to 1.5
- ssm_state: float32 [128, 16, 8192], P('grp', None, 'chan'), may hold values from -6 to 6
- out_proj: bfloat16 [8192, 4096], P('chan'), may hold values from -0.0625 to 0.0625
- router: bfloat16 [4096, 4], P('chan'), may hold values from -0.09375 to 0.09375
- expert_ids: int32 [128, 2], P('grp'), may hold values from 0 to 3, all different within a row; in each aligned block of 32 rows (0 to 31, 32 to 63, ...) at most 24 rows name the same one
- expert_gate: bfloat16 [4, 4096, 16384], P('grp', None, 'chan'), may hold values from -0.09375 to 0.09375
- expert_up: bfloat16 [4, 4096, 16384], P('grp', None, 'chan'), may hold values from -0.09375 to 0.09375
- expert_down: bfloat16 [4, 16384, 4096], P('grp', 'chan'), may hold values from -0.046875 to 0.046875
Outputs:
- layer_out: bfloat16 [128, 4096], P('grp', 'chan')
- new_state: float32 [128, 16, 8192], P('grp', None, 'chan')
Inputs may be any that keep to these rules, and one draw needn't show every extreme that they name: `expert_ids`: each request names two different experts; among the 32 requests of one group no expert is named more than 24 times, and in some group some expert is named exactly 24 times.
All inputs are finite; a program needn't handle non-finite values.
Results may differ from a plain program's by a relative error of at most 0.0056.
The roundings to bfloat16 on the way count: a program that leaves them out, or rounds other values in their place, can miss the bound.
Values may be sent and summed in bfloat16 or wider, within the bound.
A program may use at most 192 MiB of HBM per device.

v0:
```python
import jax
import jax.numpy as jnp
from jax import lax
from jax.sharding import PartitionSpec as P

EPSILON = 1e-06


def per_device(
    residual,
    conv_input,
    gate_input,
    conv_state,
    conv_weight,
    conv_bias,
    state_proj,
    step_proj,
    step_bias,
    decay_rate,
    skip_gain,
    ssm_state,
    out_proj,
    router,
    expert_ids,
    expert_gate,
    expert_up,
    expert_down,
):
    row_count = residual.shape[0]
    part_width = residual.shape[1]
    groups = lax.axis_size("grp")
    channels = lax.axis_size("chan")
    full_width = part_width * channels
    step_rank = step_proj.shape[0]
    nstates = decay_rate.shape[0]
    capacity = 3 * row_count // 4
    experts = router.shape[1]
    sharers = groups // experts
    window = conv_state.astype(jnp.float32)
    convolved = (
        conv_weight[0] * window[:, 0]
        + conv_weight[1] * window[:, 1]
        + conv_weight[2] * window[:, 2]
        + conv_weight[3] * conv_input.astype(jnp.float32)
        + conv_bias
    )
    inner_act = jax.nn.silu(convolved).astype(jnp.bfloat16)
    projected = lax.psum(jnp.dot(inner_act, state_proj, preferred_element_type=jnp.float32), "chan")
    step_raw = projected[:, :step_rank]
    input_mix = projected[:, step_rank : step_rank + nstates]
    output_mix = projected[:, step_rank + nstates :]
    step_norm = (
        step_raw * lax.rsqrt(jnp.mean(step_raw * step_raw, axis=1, keepdims=True) + EPSILON)
    ).astype(jnp.bfloat16)
    step_size = jax.nn.softplus(
        jnp.dot(step_norm, step_proj, preferred_element_type=jnp.float32) + step_bias
    )
    inner_wide = inner_act.astype(jnp.float32)
    decay_factor = jnp.exp(-step_size[:, None, :] * decay_rate[None, :, :])
    new_state = (
        decay_factor * ssm_state + (step_size * inner_wide)[:, None, :] * input_mix[:, :, None]
    )
    readout = jnp.sum(output_mix[:, :, None] * new_state, axis=1) + skip_gain * inner_wide
    gated_out = (readout * jax.nn.silu(gate_input.astype(jnp.float32))).astype(jnp.bfloat16)
    columns = out_proj
    mixer_part = lax.psum_scatter(
        lax.dot_general(
            columns, gated_out, (((0,), (1,)), ((), ())), preferred_element_type=jnp.float32
        ),
        "chan",
        scatter_dimension=0,
        tiled=True,
    )
    hidden_mid = residual.astype(jnp.float32) + mixer_part.T
    squares = jnp.sum(hidden_mid * hidden_mid, axis=1)
    router_wide = router.astype(jnp.float32)
    sum_squares = lax.psum(squares, "chan")
    inv_rms = lax.rsqrt(sum_squares / full_width + EPSILON)
    logits = lax.psum(
        jnp.dot(hidden_mid * inv_rms[:, None], router_wide, precision=lax.Precision.HIGHEST), "chan"
    )
    normed = (hidden_mid * inv_rms[:, None]).astype(jnp.bfloat16)
    labels = jnp.arange(experts, dtype=jnp.int32)
    chosen = jnp.sum(
        logits[:, None, :] * (expert_ids[:, :, None] == labels).astype(jnp.float32), axis=2
    )
    weight_first = jax.nn.sigmoid(chosen[:, 0] - chosen[:, 1])
    weight_second = 1.0 - weight_first
    flat_ids = expert_ids.reshape(-1)
    matches = (flat_ids[:, None] == labels).astype(jnp.int32)
    position = jnp.sum((jnp.cumsum(matches, axis=0) - matches) * matches, axis=1)
    target = flat_ids * capacity + position
    placing = (jnp.arange(experts * capacity, dtype=jnp.int32)[:, None] == target[None, :]).astype(
        jnp.bfloat16
    )
    repeated = jnp.repeat(normed, 2, axis=0)
    outgoing = jnp.dot(placing, repeated, preferred_element_type=jnp.float32).astype(jnp.bfloat16)
    copies = jnp.repeat(outgoing.reshape(experts, capacity, part_width), sharers, axis=0)
    incoming = lax.all_to_all(copies, "grp", split_axis=0, concat_axis=0, tiled=True)
    portion = lax.all_gather(
        incoming.reshape(groups * capacity, part_width), "chan", axis=1, tiled=True
    )
    gate_part = expert_gate[0]
    up_part = expert_up[0]
    gate_sum = jnp.dot(portion, gate_part, preferred_element_type=jnp.float32)
    up_sum = jnp.dot(portion, up_part, preferred_element_type=jnp.float32)
    hidden = (jax.nn.silu(gate_sum) * up_sum).astype(jnp.bfloat16)
    columns = expert_down[0]
    summed = lax.psum_scatter(
        lax.dot_general(
            columns, hidden, (((0,), (1,)), ((), ())), preferred_element_type=jnp.float32
        ),
        "chan",
        scatter_dimension=0,
        tiled=True,
    )
    answer = summed.T.astype(jnp.bfloat16)
    returned = lax.all_to_all(
        answer.reshape(groups, capacity, part_width), "grp", split_axis=0, concat_axis=0, tiled=True
    )
    combined = jnp.sum(
        returned.astype(jnp.float32).reshape(experts, sharers, capacity, part_width), axis=1
    )
    answers = lax.dot_general(
        placing.astype(jnp.float32),
        combined.reshape(experts * capacity, part_width),
        (((0,), (0,)), ((), ())),
        precision=lax.Precision.HIGHEST,
        preferred_element_type=jnp.float32,
    ).reshape(row_count, 2, part_width)
    layer_out = (
        hidden_mid + weight_first[:, None] * answers[:, 0] + weight_second[:, None] * answers[:, 1]
    ).astype(jnp.bfloat16)
    return (layer_out, new_state)


def solution(mesh):
    return jax.shard_map(
        per_device,
        mesh=mesh,
        in_specs=(
            P("grp", "chan"),
            P("grp", "chan"),
            P("grp", "chan"),
            P("grp", None, "chan"),
            P(None, "chan"),
            P("chan"),
            P("chan", None),
            P(None, "chan"),
            P("chan"),
            P(None, "chan"),
            P("chan"),
            P("grp", None, "chan"),
            P("chan", None),
            P("chan", None),
            P("grp", None),
            P("grp", None, "chan"),
            P("grp", None, "chan"),
            P("grp", "chan", None),
        ),
        out_specs=(P("grp", "chan"), P("grp", None, "chan")),
        check_vma=False,
    )
```

profile of v0, /device:TPU:0, one launch (start us, length us, event | category | flops | bytes accessed | tf_op | source)
XLA Modules:
  0.0 196.5 jit_solution(4262304531958366713)
XLA Ops:
  7.2 0.0 copy-start
  7.2 0.0 reduce-scatter.3.cloned.1.call-start
  7.2 0.9 fusion.51
  8.1 1.0 convert_element_type.51
  9.1 0.9 multiply_convert_fusion
  10.0 0.0 copy-done
  10.0 0.3 fusion.52
  10.3 30.7 %psum.21 = f32[32,288]{1,0:T(8,128)S(1)} all-reduce(f32[32,288]{1,0:T(8,128)S(1)} %fusion.52), channel_id=1, replica_groups=mesh['chan'=8,'grp'=4] {'chan'}, use_global_device_ids=true, to_apply=%region_0.1 | all-reduce | flops 9216 | bytes 73728 | tf_op jit(solution)/shard_map/psum | solution.py:48
  41.0 0.1 multiply_reduce_fusion.2
  41.1 0.1 fusion.50
  41.2 1.3 fusion.49
  42.6 3.8 %multiply_reduce_fusion = (f32[32,1024]{1,0:T(8,128)S(1)}, f32[32,16,1024]{2,1,0:T(8,128)}) fusion(f32[32,16]{1,0:T(8,128)S(1)} %get-tuple-element.9, f32[32,16]{1,0:T(8,128)S(1)} %get-tuple-element.8, f32[32,1024]{1,0:T(8,128)S(1)} %get-tuple-element.7, f32[32,16,1024]{2,1,0:T(8,128)} %param.29, f32[16,1024]{1,0:T(8,128)} %param.27, ...), kind=kLoop, calls=%fused_computation.10 | loop fusion | flops 3112960 | bytes 4657152 | tf_op jit(solution)/shard_map/reduce_sum | solution.py:63
  46.3 0.0 copy-start.5
  46.3 0.0 copy-start.3
  46.3 5.8 %convolution_bitcast_fusion = f32[4096,32]{0,1:T(8,128)} fusion(bf16[1024,4096]{1,0:T(8,128)(2,1)} %param.30, f32[32,1024]{1,0:T(8,128)S(1)} %get-tuple-element.4, bf16[32,1024]{1,0:T(8,128)(2,1)S(1)} %multiply_convert_fusion, bf16[32,1024]{1,0:T(8,128)(2,1)} %param.20, f32[1024]{0:T(1024)} %param.28), kind=kOutput, calls=%fused_computation.7 | convolution fusion | flops 268763136 | bytes 9179136 | tf_op jit(solution)/shard_map/dot_general | solution.py:67
  52.1 0.0 reduce-scatter.3.cloned.1.call-update
  52.1 0.0 reduce-scatter.5.cloned.1.call-start
  52.2 0.0 copy-done.5
  52.2 0.1 copy.27
  52.3 0.1 reshape.78
  52.4 0.1 fusion.41
  52.5 0.1 reduce_window_sum.11
  52.6 0.2 select_reduce_fusion
  52.8 28.7 %reduce-scatter.3.cloned.1.call-done = f32[512,32]{0,1:T(8,128)} async-done(((f32[4096,32]{0,1:T(8,128)}), f32[512,32]{0,1:T(8,128)}) %reduce-scatter.3.cloned.1.call-update) | async-done | bytes 65552 | tf_op jit(solution)/shard_map/reduce_scatter | solution.py:66
  81.5 0.0 copy-done.3
  81.5 1.0 multiply_reduce_fusion.1
  82.4 13.7 %psum.22 = f32[32]{0:T(128)S(1)} all-reduce(f32[32]{0:T(128)S(1)} %multiply_reduce_fusion.1), channel_id=1, replica_groups=mesh['chan'=8,'grp'=4] {'chan'}, use_global_device_ids=true, to_apply=%region_5.6 | all-reduce | flops 32 | bytes 256 | tf_op jit(solution)/shard_map/psum | solution.py:77
  96.1 0.9 multiply_convert_fusion.1
  97.1 0.1 convolution_convert_fusion
  97.3 8.6 %all_to_all.10 = bf16[4,24,512]{2,1,0:T(8,128)(2,1)S(1)} all-to-all(bf16[4,24,512]{2,1,0:T(8,128)(2,1)S(1)} %bitcast.102), channel_id=1, replica_groups=mesh['chan'=8,'grp'=4] {'grp'}, dimensions={0} | all-to-all | bytes 196608 | tf_op jit(solution)/shard_map/all_to_all | solution.py:99
  105.9 15.8 %all_gather.3 = bf16[96,4096]{1,0:T(8,128)(2,1)S(1)} all-gather(bf16[96,512]{1,0:T(8,128)(2,1)S(1)} %bitcast.103), channel_id=1, replica_groups=mesh['chan'=8,'grp'=4] {'chan'}, dimensions={1}, use_global_device_ids=true | all-gather | bytes 884736 | tf_op jit(solution)/shard_map/all_gather | solution.py:100
  121.7 8.5 %fusion.4 = f32[96,2048]{1,0:T(8,128)S(1)} fusion(bf16[96,4096]{1,0:T(8,128)(2,1)S(1)} %all_gather.3, bf16[1,4096,2048]{2,1,0:T(8,128)(2,1)} %param.33), kind=kOutput, calls=%fused_computation.4 | convolution fusion | flops 1610612736 | bytes 18350080 | tf_op jit(solution)/shard_map/dot_general | solution.py:105
  130.2 0.0 copy-start.2
  130.2 0.0 copy-start.4
  130.2 0.0 copy-start.1
  130.3 17.2 %fusion.6 = f32[4096,96]{0,1:T(8,128)} fusion(bf16[1,2048,4096]{2,1,0:T(8,128)(2,1)} %param.35, bf16[96,4096]{1,0:T(8,128)(2,1)S(1)} %all_gather.3, bf16[1,4096,2048]{2,1,0:T(8,128)(2,1)} %param.34, f32[96,2048]{1,0:T(8,128)S(1)} %fusion.4), kind=kOutput, calls=%fused_computation.6 | convolution fusion | flops 3222405120 | bytes 36700160 | tf_op jit(solution)/shard_map/dot_general | solution.py:110
  147.5 0.0 reduce-scatter.5.cloned.1.call-update
  147.5 0.1 iota_compare_fusion.3
  147.6 0.0 copy-done.2
  147.6 0.0 copy-done.4
  147.7 0.2 fusion.39
  147.9 14.4 %psum.23 = f32[32,4]{0,1:T(4,128)S(1)} all-reduce(f32[32,4]{0,1:T(4,128)S(1)} %fusion.39), channel_id=1, replica_groups=mesh['chan'=8,'grp'=4] {'chan'}, use_global_device_ids=true, to_apply=%region_6.7 | all-reduce | flops 128 | bytes 1024 | tf_op jit(solution)/shard_map/psum | solution.py:79
  162.3 16.7 %reduce-scatter.5.cloned.1.call-done = f32[512,96]{0,1:T(8,128)} async-done(((f32[4096,96]{0,1:T(8,128)}), f32[512,96]{0,1:T(8,128)}) %reduce-scatter.5.cloned.1.call-update) | async-done | bytes 196624 | tf_op jit(solution)/shard_map/reduce_scatter | solution.py:109
  179.0 1.6 convert_element_type.62
  180.5 3.3 %all-to-all-start.1 = ((bf16[4,24,512]{2,1,0:T(8,128)(2,1)}), bf16[4,24,512]{2,1,0:T(8,128)(2,1)S(1)}, u32[]{:S(2)}, u32[]{:S(2)}) async-start(bf16[4,24,512]{2,1,0:T(8,128)(2,1)} %bitcast.17), calls=%async_computation.3 | async-start | bytes 196608 | tf_op jit(solution)/shard_map/all_to_all | solution.py:118
  183.8 4.9 %all-to-all-done.1 = bf16[4,24,512]{2,1,0:T(8,128)(2,1)S(1)} async-done(((bf16[4,24,512]{2,1,0:T(8,128)(2,1)}), bf16[4,24,512]{2,1,0:T(8,128)(2,1)S(1)}, u32[]{:S(2)}, u32[]{:S(2)}) %all-to-all-start.1) | async-done | bytes 98336 | tf_op jit(solution)/shard_map/all_to_all | solution.py:118
  188.8 0.1 fusion.43
  188.9 0.7 fusion.34
  189.6 0.0 copy-done.1
  (8 shorter events, 0.1 us)
Async XLA Ops:
  7.2 2.8 %copy-start = (bf16[1024,288]{0,1:T(8,128)(2,1)S(1)}, bf16[1024,288]{0,1:T(8,128)(2,1)}, u32[]{:S(2)}) copy-start(bf16[1024,288]{0,1:T(8,128)(2,1)} %param.24) | copy-start | bytes 1769476
  7.2 74.3 %reduce-scatter.3.cloned.1.call-start = ((), (), s32[]{:S(2)}) async-start(), calls=%async_computation.4 | async-start | bytes 589824 | tf_op jit(solution)/shard_map/reduce_scatter | solution.py:66
  46.3 5.9 %copy-start.5 = (s32[32,2]{0,1:T(2,128)S(1)}, s32[32,2]{0,1:T(2,128)}, u32[]{:S(2)}) copy-start(s32[32,2]{0,1:T(2,128)} %param.32) | copy-start | bytes 772
  46.3 35.1 %copy-start.3 = (bf16[32,512]{1,0:T(8,128)(2,1)S(1)}, bf16[32,512]{1,0:T(8,128)(2,1)}, u32[]{:S(2)}) copy-start(bf16[32,512]{1,0:T(8,128)(2,1)} %param.18) | copy-start | bytes 98308
  52.1 126.8 %reduce-scatter.5.cloned.1.call-start = ((), (), s32[]{:S(2)}) async-start(), calls=%async_computation.5 | async-start | bytes 1769472 | tf_op jit(solution)/shard_map/reduce_scatter | solution.py:109
  130.2 17.4 %copy-start.2 = (f32[512,32]{0,1:T(8,128)S(1)}, f32[512,32]{0,1:T(8,128)}, u32[]{:S(2)}) copy-start(f32[512,32]{0,1:T(8,128)} %reduce-scatter.3.cloned.1.call-done) | copy-start | bytes 196612
  130.2 17.4 %copy-start.4 = (bf16[512,4]{0,1:T(4,128)(2,1)S(1)}, bf16[512,4]{0,1:T(4,128)(2,1)}, u32[]{:S(2)}) copy-start(bf16[512,4]{0,1:T(4,128)(2,1)} %param.31) | copy-start | bytes 12292
  130.2 59.4 %copy-start.1 = (bf16[1024,288]{0,1:T(8,128)(2,1)S(1)}, bf16[1024,288]{0,1:T(8,128)(2,1)}, u32[]{:S(2)}) copy-start(bf16[1024,288]{0,1:T(8,128)(2,1)} %param.24) | copy-start | bytes 1769476
  180.5 8.3 %all-to-all-start.1 = ((bf16[4,24,512]{2,1,0:T(8,128)(2,1)}), bf16[4,24,512]{2,1,0:T(8,128)(2,1)S(1)}, u32[]{:S(2)}, u32[]{:S(2)}) async-start(bf16[4,24,512]{2,1,0:T(8,128)(2,1)} %bitcast.17), calls=%async_computation.3 | async-start | bytes 196608 | tf_op jit(solution)/shard_map/all_to_all | solution.py:118
Sparse Core Ops, SparseCore 0:
  52.3 29.1 reduce-scatter.2
  147.6 31.2 reduce-scatter.4
where the time goes:
time: 197 us; the launch traced here: 196 us
  blocking collectives  83.2 us (42%)
  waiting for transfers between devices  50.3 us (26%)
  matrix products  33.7 us (17%)
  between operations  14.2 us (7%)
  other arithmetic  10.4 us (5%)
  starting transfers between devices  3.4 us (2%)
    psum x1, blocking collectives, per_device(): lax.psum(jnp.dot(inner_act, state_proj, preferred_element_type=jnp.float3...  30.7 us
    reduce_scatter x1, waiting for transfers between devices, per_device(): lax.psum_scatter(lax.dot_general(columns, gated_out, (((0,), (1,)), ((),...  28.7 us
    dot_general x1, matrix products, per_device(): lax.dot_general(columns, hidden, (((0,), (1,)), ((), ())), preferred_elem...  17.2 us
    reduce_scatter x1, waiting for transfers between devices, per_device(): lax.psum_scatter(lax.dot_general(columns, hidden, (((0,), (1,)), ((), ())...  16.7 us
    all_gather x1, blocking collectives, per_device(): lax.all_gather(incoming.reshape(groups * capacity, part_width), 'chan', a...  15.8 us
    psum x1, blocking collectives, per_device(): lax.psum(jnp.dot(hidden_mid * inv_rms[:, None], router_wide, precision=la...  14.4 us
    psum x1, blocking collectives, per_device(): sum_squares = lax.psum(squares, 'chan')  13.7 us
    all_to_all x1, blocking collectives, per_device(): lax.all_to_all(copies, 'grp', split_axis=0, concat_axis=0, tiled=True)  8.62 us
  transfers between devices with their start and end apart: 3, of which 3 were waited for; matrix products, arithmetic and copies ran while one was open for 0% of the time, Pallas kernels for 0%

commit v1 on v0

--- a/solution.py
+++ b/solution.py
@@ -1,9 +1,25 @@
+import functools
 import jax
 import jax.numpy as jnp
 from jax import lax
 from jax.sharding import PartitionSpec as P
 
 EPSILON = 1e-06
+
+
+def raise_the_samples_all(local_x, mesh_dim):
+    high, block_last = (lax.axis_size(mesh_dim), lax.axis_index(mesh_dim))
+    b_now, small = (local_x, 1)
+    while small < high:
+        wide_out = lax.ppermute(b_now, mesh_dim, tuple(((s, s ^ small) for s in range(high))))
+        carry_in = jnp.concatenate([b_now, wide_out], axis=1)
+        piece_next = jnp.concatenate([wide_out, b_now], axis=1)
+        b_now = jnp.where(block_last & small == 0, carry_in, piece_next)
+        small = 2 * small
+    return b_now
+
+
+manage_bench = functools.partial(raise_the_samples_all, mesh_dim="chan")
 
 
 def per_device(
@@ -97,9 +113,7 @@
     outgoing = jnp.dot(placing, repeated, preferred_element_type=jnp.float32).astype(jnp.bfloat16)
     copies = jnp.repeat(outgoing.reshape(experts, capacity, part_width), sharers, axis=0)
     incoming = lax.all_to_all(copies, "grp", split_axis=0, concat_axis=0, tiled=True)
-    portion = lax.all_gather(
-        incoming.reshape(groups * capacity, part_width), "chan", axis=1, tiled=True
-    )
+    portion = manage_bench(incoming.reshape(groups * capacity, part_width))
     gate_part = expert_gate[0]
     up_part = expert_up[0]
     gate_sum = jnp.dot(portion, gate_part, preferred_element_type=jnp.float32)

time: 197 us -> 207 us (1.051)
  waiting for transfers between devices: 50.3 us -> 78.4 us
  blocking collectives: 83.2 us -> 66.7 us
    ppermute x0 -> x3, waiting for transfers between devices: none -> 27.9 us  [raise_the_samples_all(): lax.ppermute(b_now, mesh_dim, tuple(((s, s ^ small) for s in range(high))))]
    all_gather x1 -> x0, blocking collectives: 15.8 us -> none  [per_device(): lax.all_gather(incoming.reshape(groups * capacity, part_width), 'chan', a...]
  transfers between devices with their start and end apart: 3 -> 6, of which waited for: 3 -> 6; matrix products, arithmetic and copies ran while one was open for 0% -> 0% of each run, Pallas kernels for 0% -> 0%
where the time goes in v1:
time: 207 us
  waiting for transfers between devices  78.4 us (38%)
  blocking collectives  66.7 us (32%)
  matrix products  33.3 us (16%)
  between operations  14.3 us (7%)
  other arithmetic  8.96 us (4%)
  starting transfers between devices  3.71 us (2%)
    psum x1, blocking collectives, per_device(): lax.psum(jnp.dot(inner_act, state_proj, preferred_element_type=jnp.float3...  30.7 us
    reduce_scatter x1, waiting for transfers between devices, per_device(): lax.psum_scatter(lax.dot_general(columns, gated_out, (((0,), (1,)), ((),...  28.7 us
    ppermute x3, waiting for transfers between devices, raise_the_samples_all(): lax.ppermute(b_now, mesh_dim, tuple(((s, s ^ small) for s in range(high))))  27.9 us
    dot_general x1, matrix products, per_device(): lax.dot_general(columns, hidden, (((0,), (1,)), ((), ())), preferred_elem...  17.3 us
    reduce_scatter x1, waiting for transfers between devices, per_device(): lax.psum_scatter(lax.dot_general(columns, hidden, (((0,), (1,)), ((), ())...  16.9 us
    psum x1, blocking collectives, per_device(): sum_squares = lax.psum(squares, 'chan')  13.7 us
    psum x1, blocking collectives, per_device(): lax.psum(jnp.dot(hidden_mid * inv_rms[:, None], router_wide, precision=la...  13.6 us
    all_to_all x1, blocking collectives, per_device(): lax.all_to_all(copies, 'grp', split_axis=0, concat_axis=0, tiled=True)  8.67 us
  transfers between devices with their start and end apart: 6, of which 6 were waited for; matrix products, arithmetic and copies ran while one was open for 0% of the time, Pallas kernels for 0%

profile of v1, /device:TPU:0, one launch (start us, length us, event | category | flops | bytes accessed | tf_op | source)
XLA Modules:
  0.0 206.7 jit_solution(4382513512648326720)
XLA Ops:
  7.2 0.0 copy-start
  7.2 0.0 copy-start.4
  7.2 0.0 copy-start.7
  7.2 0.0 copy-start.2
  7.2 0.0 reduce-scatter.3.cloned.1.call-start
  7.3 0.9 fusion.50
  8.2 1.0 convert_element_type.51
  9.2 0.9 multiply_convert_fusion.2
  10.1 0.0 copy-done
  10.1 0.3 fusion.51
  10.4 30.7 %psum.21 = f32[32,288]{1,0:T(8,128)S(1)} all-reduce(f32[32,288]{1,0:T(8,128)S(1)} %fusion.51), channel_id=1, replica_groups=mesh['chan'=8,'grp'=4] {'chan'}, use_global_device_ids=true, to_apply=%region_0.1 | all-reduce | flops 9216 | bytes 73728 | tf_op jit(solution)/shard_map/psum | solution.py:64
  41.1 0.1 multiply_reduce_fusion.2
  41.2 0.1 fusion.49
  41.3 0.0 copy-done.4
  41.3 1.0 fusion.48
  42.3 0.0 copy-done.7
  42.3 0.0 copy-done.2
  42.3 0.0 copy-start.6
  42.3 0.0 copy-start.8
  42.3 2.2 %multiply_reduce_fusion = (f32[32,1024]{1,0:T(8,128)S(1)}, f32[32,16,1024]{2,1,0:T(8,128)}) fusion(f32[32,16]{1,0:T(8,128)S(1)} %get-tuple-element.9, f32[32,16]{1,0:T(8,128)S(1)} %get-tuple-element.8, f32[32,1024]{1,0:T(8,128)S(1)} %get-tuple-element.7, f32[32,16,1024]{2,1,0:T(8,128)S(1)} %copy-done.2, f32[16,1024]{1,0:T(8,128)S(1)} %copy-done.7, ...), kind=kLoop, calls=%fused_computation.8 | loop fusion | flops 3112960 | bytes 4657152 | tf_op jit(solution)/shard_map/reduce_sum | solution.py:79
  44.5 0.0 copy-done.6
  44.5 0.0 copy-done.8
  44.5 5.7 %convolution_bitcast_fusion = f32[4096,32]{0,1:T(8,128)} fusion(bf16[1024,4096]{1,0:T(8,128)(2,1)} %param.30, f32[32,1024]{1,0:T(8,128)S(1)} %get-tuple-element.4, bf16[32,1024]{1,0:T(8,128)(2,1)S(1)} %multiply_convert_fusion.2, bf16[32,1024]{1,0:T(8,128)(2,1)S(1)} %copy-done.6, f32[1024]{0:T(1024)S(1)} %copy-done.8), kind=kOutput, calls=%fused_computation.7 | convolution fusion | flops 268763136 | bytes 9179136 | tf_op jit(solution)/shard_map/dot_general | solution.py:83
  50.3 0.0 reduce-scatter.3.cloned.1.call-update
  50.3 0.0 reduce-scatter.5.cloned.1.call-start
  50.3 0.0 copy-done.10
  50.4 0.1 copy.27
  50.4 0.1 reshape.78
  50.5 0.1 fusion.37
  50.6 0.1 reduce_window_sum.11
  50.7 0.2 select_reduce_fusion
  50.9 28.7 %reduce-scatter.3.cloned.1.call-done = f32[512,32]{0,1:T(8,128)} async-done(((f32[4096,32]{0,1:T(8,128)}), f32[512,32]{0,1:T(8,128)}) %reduce-scatter.3.cloned.1.call-update) | async-done | bytes 65552 | tf_op jit(solution)/shard_map/reduce_scatter | solution.py:82
  79.6 0.0 copy-done.5
  79.6 1.0 multiply_reduce_fusion.1
  80.5 13.7 %psum.22 = f32[32]{0:T(128)S(1)} all-reduce(f32[32]{0:T(128)S(1)} %multiply_reduce_fusion.1), channel_id=1, replica_groups=mesh['chan'=8,'grp'=4] {'chan'}, use_global_device_ids=true, to_apply=%region_5.6 | all-reduce | flops 32 | bytes 256 | tf_op jit(solution)/shard_map/psum | solution.py:93
  94.2 0.9 multiply_convert_fusion.3
  95.2 0.2 convolution_convert_fusion
  95.4 8.7 %all_to_all.10 = bf16[4,24,512]{2,1,0:T(8,128)(2,1)S(1)} all-to-all(bf16[4,24,512]{2,1,0:T(8,128)(2,1)S(1)} %bitcast.98), channel_id=1, replica_groups=mesh['chan'=8,'grp'=4] {'grp'}, dimensions={0} | all-to-all | bytes 196608 | tf_op jit(solution)/shard_map/all_to_all | solution.py:115
  104.1 0.0 collective-permute-start
  104.1 1.3 collective-permute-done
  105.4 0.1 maximum_select_fusion.2
  105.4 0.1 collective-permute-start.1
  105.5 6.9 %collective-permute-done.1 = bf16[96,1024]{1,0:T(8,128)(2,1)S(1)} collective-permute-done((bf16[96,1024]{1,0:T(8,128)(2,1)S(1)}, bf16[96,1024]{1,0:T(8,128)(2,1)S(1)}, u32[]{:S(2)}, u32[]{:S(2)}) %collective-permute-start.1) | collective-permute-done | bytes 196640 | tf_op jit(solution)/shard_map/ppermute | solution.py:14
  112.5 0.1 maximum_select_fusion.1
  112.6 0.1 collective-permute-start.2
  112.6 19.7 %collective-permute-done.2 = bf16[96,2048]{1,0:T(8,128)(2,1)S(1)} collective-permute-done((bf16[96,2048]{1,0:T(8,128)(2,1)S(1)}, bf16[96,2048]{1,0:T(8,128)(2,1)S(1)}, u32[]{:S(2)}, u32[]{:S(2)}) %collective-permute-start.2) | collective-permute-done | bytes 393248 | tf_op jit(solution)/shard_map/ppermute | solution.py:14
  132.3 8.5 %fusion.2 = f32[96,2048]{1,0:T(8,128)S(1)} fusion(bf16[1,4096,2048]{2,1,0:T(8,128)(2,1)} %param.34, bf16[96,2048]{1,0:T(8,128)(2,1)S(1)} %collective-permute-done.2, bf16[96,2048]{1,0:T(8,128)(2,1)S(1)} %maximum_select_fusion.1, pred[]{:T(512)S(6)} %eq.73), kind=kOutput, calls=%fused_computation.2 | convolution fusion | flops 1614151680 | bytes 18350080 | tf_op jit(solution)/shard_map/dot_general | solution.py:120
  140.8 0.0 copy-start.3
  140.8 0.0 copy-start.9
  140.8 0.0 copy-start.1
  140.9 17.3 %fusion.6 = f32[4096,96]{0,1:T(8,128)} fusion(bf16[1,2048,4096]{2,1,0:T(8,128)(2,1)} %param.35, f32[96,2048]{1,0:T(8,128)S(1)} %fusion.2, bf16[1,4096,2048]{2,1,0:T(8,128)(2,1)} %param.33, bf16[96,2048]{1,0:T(8,128)(2,1)S(1)} %collective-permute-done.2, bf16[96,2048]{1,0:T(8,128)(2,1)S(1)} %maximum_select_fusion.1, pred[]{:T(512)S(6)} %eq.73), kind=kOutput, calls=%fused_computation.6 | convolution fusion | flops 3225944064 | bytes 36700160 | tf_op jit(solution)/shard_map/dot_general | solution.py:124
  158.2 0.0 reduce-scatter.5.cloned.1.call-update
  158.2 0.1 iota_compare_fusion.3
  158.3 0.0 copy-done.3
  158.3 0.0 copy-done.9
  158.3 0.2 fusion.35
  158.5 13.6 %psum.23 = f32[32,4]{0,1:T(4,128)S(1)} all-reduce(f32[32,4]{0,1:T(4,128)S(1)} %fusion.35), channel_id=1, replica_groups=mesh['chan'=8,'grp'=4] {'chan'}, use_global_device_ids=true, to_apply=%region_6.7 | all-reduce | flops 128 | bytes 1024 | tf_op jit(solution)/shard_map/psum | solution.py:95
  172.2 16.9 %reduce-scatter.5.cloned.1.call-done = f32[512,96]{0,1:T(8,128)} async-done(((f32[4096,96]{0,1:T(8,128)}), f32[512,96]{0,1:T(8,128)}) %reduce-scatter.5.cloned.1.call-update) | async-done | bytes 196624 | tf_op jit(solution)/shard_map/reduce_scatter | solution.py:123
  189.0 1.6 convert_element_type.62
  190.6 3.5 %all-to-all-start.1 = ((bf16[4,24,512]{2,1,0:T(8,128)(2,1)}), bf16[4,24,512]{2,1,0:T(8,128)(2,1)S(1)}, u32[]{:S(2)}, u32[]{:S(2)}) async-start(bf16[4,24,512]{2,1,0:T(8,128)(2,1)} %bitcast.17), calls=%async_computation.3 | async-start | bytes 196608 | tf_op jit(solution)/shard_map/all_to_all | solution.py:132
  194.1 4.9 %all-to-all-done.1 = bf16[4,24,512]{2,1,0:T(8,128)(2,1)S(1)} async-done(((bf16[4,24,512]{2,1,0:T(8,128)(2,1)}), bf16[4,24,512]{2,1,0:T(8,128)(2,1)S(1)}, u32[]{:S(2)}, u32[]{:S(2)}) %all-to-all-start.1) | async-done | bytes 98336 | tf_op jit(solution)/shard_map/all_to_all | solution.py:132
  199.0 0.1 fusion.39
  199.2 0.7 fusion.30
  199.9 0.0 copy-done.1
  (10 shorter events, 0.1 us)
Async XLA Ops:
  7.2 3.0 %copy-start = (bf16[1024,288]{0,1:T(8,128)(2,1)S(1)}, bf16[1024,288]{0,1:T(8,128)(2,1)}, u32[]{:S(2)}) copy-start(bf16[1024,288]{0,1:T(8,128)(2,1)} %param.24) | copy-start | bytes 1769476
  7.2 34.1 %copy-start.4 = (bf16[256,1024]{1,0:T(8,128)(2,1)S(1)}, bf16[256,1024]{1,0:T(8,128)(2,1)}, u32[]{:S(2)}) copy-start(bf16[256,1024]{1,0:T(8,128)(2,1)} %param.25) | copy-start | bytes 1572868
  7.2 35.1 %copy-start.7 = (f32[16,1024]{1,0:T(8,128)S(1)}, f32[16,1024]{1,0:T(8,128)}, u32[]{:S(2)}) copy-start(f32[16,1024]{1,0:T(8,128)} %param.27) | copy-start | bytes 196612
  7.2 35.1 %copy-start.2 = (f32[32,16,1024]{2,1,0:T(8,128)S(1)}, f32[32,16,1024]{2,1,0:T(8,128)}, u32[]{:S(2)}) copy-start(f32[32,16,1024]{2,1,0:T(8,128)} %param.29) | copy-start | bytes 6291460
  7.2 72.4 %reduce-scatter.3.cloned.1.call-start = ((), (), s32[]{:S(2)}) async-start(), calls=%async_computation.4 | async-start | bytes 589824 | tf_op jit(solution)/shard_map/reduce_scatter | solution.py:82
  42.3 2.2 %copy-start.6 = (bf16[32,1024]{1,0:T(8,128)(2,1)S(1)}, bf16[32,1024]{1,0:T(8,128)(2,1)}, u32[]{:S(2)}) copy-start(bf16[32,1024]{1,0:T(8,128)(2,1)} %param.20) | copy-start | bytes 196612
  42.3 2.2 %copy-start.8 = (f32[1024]{0:T(1024)S(1)}, f32[1024]{0:T(1024)}, u32[]{:S(2)}) copy-start(f32[1024]{0:T(1024)} %param.28) | copy-start | bytes 12292
  44.5 5.8 %copy-start.10 = (s32[32,2]{0,1:T(2,128)S(1)}, s32[32,2]{0,1:T(2,128)}, u32[]{:S(2)}) copy-start(s32[32,2]{0,1:T(2,128)} %param.32) | copy-start | bytes 772
  44.5 35.1 %copy-start.5 = (bf16[32,512]{1,0:T(8,128)(2,1)S(1)}, bf16[32,512]{1,0:T(8,128)(2,1)}, u32[]{:S(2)}) copy-start(bf16[32,512]{1,0:T(8,128)(2,1)} %param.18) | copy-start | bytes 98308
  50.3 138.8 %reduce-scatter.5.cloned.1.call-start = ((), (), s32[]{:S(2)}) async-start(), calls=%async_computation.5 | async-start | bytes 1769472 | tf_op jit(solution)/shard_map/reduce_scatter | solution.py:123
  104.1 1.3 collective-permute-start
  105.4 7.0 %collective-permute-start.1 = (bf16[96,1024]{1,0:T(8,128)(2,1)S(1)}, bf16[96,1024]{1,0:T(8,128)(2,1)S(1)}, u32[]{:S(2)}, u32[]{:S(2)}) collective-permute-start(bf16[96,1024]{1,0:T(8,128)(2,1)S(1)} %maximum_select_fusion.2), channel_id=1, source_target_pairs={{0,8},{4,12},{8,0},{12,4},{16,24},{20,28},{24,16},{28,20},{1,9},{5... | collective-permute-start | bytes 589832 | tf_op jit(solution)/shard_map/ppermute | solution.py:14
  112.6 19.7 %collective-permute-start.2 = (bf16[96,2048]{1,0:T(8,128)(2,1)S(1)}, bf16[96,2048]{1,0:T(8,128)(2,1)S(1)}, u32[]{:S(2)}, u32[]{:S(2)}) collective-permute-start(bf16[96,2048]{1,0:T(8,128)(2,1)S(1)} %maximum_select_fusion.1), channel_id=1, source_target_pairs={{0,16},{4,20},{8,24},{12,28},{16,0},{20,4},{24,8},{28,12},{1,17},{... | collective-permute-start | bytes 1179656 | tf_op jit(solution)/shard_map/ppermute | solution.py:14
  140.8 17.5 %copy-start.3 = (f32[512,32]{0,1:T(8,128)S(1)}, f32[512,32]{0,1:T(8,128)}, u32[]{:S(2)}) copy-start(f32[512,32]{0,1:T(8,128)} %reduce-scatter.3.cloned.1.call-done) | copy-start | bytes 196612
  140.8 17.5 %copy-start.9 = (bf16[512,4]{0,1:T(4,128)(2,1)S(1)}, bf16[512,4]{0,1:T(4,128)(2,1)}, u32[]{:S(2)}) copy-start(bf16[512,4]{0,1:T(4,128)(2,1)} %param.31) | copy-start | bytes 12292
  140.8 59.0 %copy-start.1 = (bf16[1024,288]{0,1:T(8,128)(2,1)S(1)}, bf16[1024,288]{0,1:T(8,128)(2,1)}, u32[]{:S(2)}) copy-start(bf16[1024,288]{0,1:T(8,128)(2,1)} %param.24) | copy-start | bytes 1769476
  190.6 8.4 %all-to-all-start.1 = ((bf16[4,24,512]{2,1,0:T(8,128)(2,1)}), bf16[4,24,512]{2,1,0:T(8,128)(2,1)S(1)}, u32[]{:S(2)}, u32[]{:S(2)}) async-start(bf16[4,24,512]{2,1,0:T(8,128)(2,1)} %bitcast.17), calls=%async_computation.3 | async-start | bytes 196608 | tf_op jit(solution)/shard_map/all_to_all | solution.py:132
Sparse Core Ops, SparseCore 0:
  50.4 29.1 reduce-scatter.2
  158.3 30.6 reduce-scatter.4
